TPU v7x, 256 devices: a whole 4x4x8 slice. The times are simulated.
256 devices in a mesh: dp: 32 (over y, z), tensor: 8 (over x, core).
Axes of the slice: x: 4, y: 4, z: 8, core: 2. Of those that a mesh axis runs over, the one named last changes fastest.
Arguments:
- activations: bfloat16 [65536, 5120], P('dp'), may hold values from -20 to 20, as said below
- out_grads: bfloat16 [65536, 2560], P('dp', 'tensor'), may hold values from -0.3125 to 0.3125, as said below
- error_memory: bfloat16 [32, 2560, 5120], P('dp', 'tensor'), may hold values from -6 to 6
- warm_start: bfloat16 [2560, 64], P('tensor'), may hold values from -6 to 6
Outputs:
- update: bfloat16 [2560, 5120], P('tensor')
- new_error: bfloat16 [32, 2560, 5120], P('dp', 'tensor')
- next_start: float32 [2560, 64], P('tensor')
Inputs may be any that keep to these rules, and one draw needn't show every extreme that they name: activations of each replica share a common part and have feature scales that differ. `out_grads`: cotangents of each replica share a common part.
All inputs are finite; a program needn't handle non-finite values.
Results may differ from a plain program's by a relative error of at most 0.007.
Values may be sent and summed in bfloat16 or wider, within the bound.
No kernel may reach another device: no remote copies, remote signals or barrier semaphores. Data moves between devices by JAX's collectives and lax.ppermute only.
A program may use at most 128 MiB of HBM per device.

v0:
```python
import jax
import jax.numpy as jnp
from jax import lax
from jax.sharding import PartitionSpec as P

CONTRACT_ROWS = (((0,), (0,)), ((), ()))


def orthonormal(sketch_part, gram_total):
    factor = jnp.linalg.cholesky(gram_total)
    return jax.scipy.linalg.solve_triangular(factor, sketch_part.T, lower=True).T


def per_device(activations, out_grads, error_memory, warm_start):
    gradient = lax.dot_general(
        out_grads, activations, CONTRACT_ROWS, preferred_element_type=jnp.float32
    )
    merged = (gradient + error_memory[0].astype(jnp.float32)).astype(jnp.bfloat16)
    sketch_local = lax.dot_general(
        merged, warm_start, CONTRACT_ROWS, preferred_element_type=jnp.float32
    )
    sketch = lax.psum(sketch_local, ("dp", "tensor"))
    gram_total = jnp.dot(sketch.T, sketch, precision=lax.Precision.HIGHEST)
    basis_half = orthonormal(sketch, gram_total).astype(jnp.bfloat16)
    coeff_local = jnp.dot(merged, basis_half, preferred_element_type=jnp.float32)
    next_start = lax.psum(coeff_local, "dp") / lax.axis_size("dp")
    start_half = next_start.astype(jnp.bfloat16)
    decoded = lax.dot_general(
        start_half, basis_half, (((1,), (1,)), ((), ())), preferred_element_type=jnp.float32
    )
    update = decoded.astype(jnp.bfloat16)
    new_error = (merged.astype(jnp.float32) - decoded).astype(jnp.bfloat16)[None]
    return (update, new_error, next_start)


def solution(mesh):
    placed = (P("dp", None), P("dp", "tensor"), P("dp", "tensor", None), P("tensor", None))
    return jax.shard_map(
        per_device,
        mesh=mesh,
        in_specs=placed,
        out_specs=(P("tensor", None), P("dp", "tensor", None), P("tensor", None)),
        check_vma=False,
    )
```

profile of v0, /device:TPU:2, one launch (start us, length us, event | category | flops | bytes accessed | tf_op | source)
XLA Modules:
  0.0 458.7 jit_solution(16130339753533579462)
XLA Ops:
  7.2 0.0 copy-start
  7.2 0.0 copy-start.4
  7.2 0.0 all-reduce.3.cloned.1.call-start
  7.2 1.3 copy-done
  8.5 11.6 %fusion = bf16[320,5120]{1,0:T(8,128)(2,1)S(1)} fusion(bf16[2048,320]{0,1:T(8,128)(2,1)S(1)} %copy-done, bf16[2048,5120]{1,0:T(8,128)(2,1)} %param.4, bf16[1,320,5120]{2,1,0:T(8,128)(2,1)} %param.6), kind=kOutput, calls=%fused_computation.1 | convolution fusion | flops 6715801600 | bytes 28835840 | tf_op jit(solution)/shard_map/dot_general | solution.py:15
  20.1 0.0 copy-start.1
  20.1 1.7 copy-done.1
  21.8 0.0 copy-done.4
  21.8 1.8 fusion.11
  23.6 0.0 all-reduce.3.cloned.1.call-update
  23.7 0.0 all-reduce.5.cloned.1.call-start
  23.7 261.5 %all-reduce.3.cloned.1.call-done = f32[5120,64]{0,1:T(8,128)} async-done(((f32[5120,64]{0,1:T(8,128)}), f32[5120,64]{0,1:T(8,128)}) %all-reduce.3.cloned.1.call-update) | async-done | bytes 1310736 | tf_op jit(solution)/shard_map/psum | solution.py:22
  285.2 0.0 copy-start.2
  285.2 3.0 fusion.9
  288.3 0.1 copy.7
  288.4 5.8 %cholesky.16 = f32[64,64]{1,0:T(8,128)S(1)} custom-call(f32[64,64]{1,0:T(8,128)S(1)} %fusion.6), custom_call_target="Cholesky" | custom-call | tf_op jit(solution)/shard_map/jit(cholesky)/cholesky | solution.py:10
  294.3 0.6 compare_reduce_fusion
  294.9 0.7 fusion.4
  295.6 4.9 %custom-call.7 = f32[1,64,64]{1,2,0:T(8,128)S(1)} custom-call(f32[1,64,64]{2,1,0:T(8,128)S(1)} %fusion.4), custom_call_target="InvertDiagBlocksLowerTriangular" | custom-call | tf_op jit(solution)/shard_map/jit(_solve_triangular)/triangular_solve | solution.py:11
  300.5 0.0 copy-done.2
  300.5 1.3 convolution_convert_fusion
  301.8 3.7 fusion.10
  305.4 0.0 all-reduce.5.cloned.1.call-update
  305.5 139.7 %all-reduce.5.cloned.1.call-done = f32[320,64]{0,1:T(8,128)} async-done(((f32[320,64]{0,1:T(8,128)}), f32[320,64]{0,1:T(8,128)}) %all-reduce.5.cloned.1.call-update) | async-done | bytes 81936 | tf_op jit(solution)/shard_map/psum | solution.py:26
  445.2 0.9 broadcast_multiply_fusion
  446.1 0.0 copy-start.3
  446.1 5.8 %fusion.1 = (bf16[1,320,5120]{2,1,0:T(8,128)(2,1)}, bf16[320,5120]{1,0:T(8,128)(2,1)}) fusion(bf16[320,5120]{1,0:T(8,128)(2,1)} %copy-done.1, bf16[5120,64]{0,1:T(8,128)(2,1)S(1)} %convolution_convert_fusion, f32[320,64]{0,1:T(8,128)S(1)} %broadcast_multiply_fusion), kind=kOutput, calls=%fused_computation.4 | convolution fusion | flops 216289280 | bytes 10567680 | tf_op jit(solution)/shard_map/dot_general | solution.py:28
  451.9 0.0 copy-done.3
  (2 shorter events, 0.0 us)
Async XLA Ops:
  7.2 1.3 copy-start
  7.2 14.6 %copy-start.4 = (bf16[320,64]{0,1:T(8,128)(2,1)S(1)}, bf16[320,64]{0,1:T(8,128)(2,1)}, u32[]{:S(2)}) copy-start(bf16[320,64]{0,1:T(8,128)(2,1)} %param.7) | copy-start | bytes 122884
  7.2 278.0 %all-reduce.3.cloned.1.call-start = ((), (), s32[]{:S(2)}) async-start(), calls=%async_computation | async-start | bytes 2621440 | tf_op jit(solution)/shard_map/psum | solution.py:22
  20.1 1.7 copy-start.1
  23.7 421.5 %all-reduce.5.cloned.1.call-start = ((), (), s32[]{:S(2)}) async-start(), calls=%async_computation.1 | async-start | bytes 196608 | tf_op jit(solution)/shard_map/psum | solution.py:26
  285.2 15.2 %copy-start.2 = (f32[5120,64]{0,1:T(8,128)S(1)}, f32[5120,64]{0,1:T(8,128)}, u32[]{:S(2)}) copy-start(f32[5120,64]{0,1:T(8,128)} %all-reduce.3.cloned.1.call-done) | copy-start | bytes 3932164
  446.1 5.8 %copy-start.3 = (f32[320,64]{0,1:T(8,128)}, f32[320,64]{0,1:T(8,128)S(1)}, u32[]{:S(2)}) copy-start(f32[320,64]{0,1:T(8,128)S(1)} %broadcast_multiply_fusion) | copy-start | bytes 245764
Sparse Core Ops, SparseCore 0:
  23.8 261.4 all-reduce.2
  305.6 139.5 all-reduce.4
where the time goes:
time: 459 us
  waiting for transfers between devices  401 us (87%)
  matrix products  27.2 us (6%)
  between operations  14.1 us (3%)
  other arithmetic  13 us (3%)
    psum x1, waiting for transfers between devices, per_device(): sketch = lax.psum(sketch_local, ('dp', 'tensor'))  262 us
    psum x1, waiting for transfers between devices, per_device(): next_start = lax.psum(coeff_local, 'dp') / lax.axis_size('dp')  140 us
    dot_general x1, matrix products, per_device(): lax.dot_general(out_grads, activations, CONTRACT_ROWS, preferred_element_...  11.6 us
  transfers between devices with their start and end apart: 2, of which 2 were waited for; matrix products, arithmetic and copies ran while one was open for 0% of the time, Pallas kernels for 0%

commit v1 on v0

v1 whole, which is shorter than its diff:
```python
import jax
import jax.numpy as jnp
from jax import lax
from jax.experimental import pallas as pl
from jax.experimental.pallas import tpu as pltpu
from jax.sharding import Mesh, PartitionSpec as P

D = 5120
C = 320
R = 64
TOK = 2048
N_DP = 32
N_X, N_Y, N_Z = 4, 4, 8
HALF = D // 2
BLK = 512
MXU = 256
PIECE = 512
PIECES = TOK // PIECE
SLOTS = 3
LANES = 128
GROUP = N_X * LANES
STEPS = D // BLK
HSTEPS = STEPS // 2
ROWS = R // N_Y
COLS = HALF // N_X
PARTS = N_X * N_Y
PAD = 384
F32, BF16 = jnp.float32, jnp.bfloat16
NT = (((1,), (1,)), ((), ()))
TN = (((0,), (0,)), ((), ()))
MIB = 1024 * 1024


def merge_body(
    core_ref, grads_hbm, tokens_hbm, memory_hbm, warm_hbm, merged_ref, send_ref, own_ref,
    grads, tokens, memory, low_rows, warm, warm_copied, grads_sem, tokens_sem, memory_sem, warm_sem,
):
    core = core_ref[0]

    def column(j):
        half = jnp.where(j < HSTEPS, 1 - core, core)
        return pl.multiple_of((half * HSTEPS + lax.rem(j, HSTEPS)) * BLK, BLK)

    def grads_copy(i):
        at = pl.ds(i * PIECE, PIECE)
        return pltpu.make_async_copy(grads_hbm.at[:, at], grads.at[:, at], grads_sem.at[i])

    def tokens_copy(j, i):
        slot, at = lax.rem(j, SLOTS), pl.ds(i * PIECE, PIECE)
        return pltpu.make_async_copy(
            tokens_hbm.at[at, pl.ds(column(j), BLK)], tokens.at[slot, at], tokens_sem.at[slot, i]
        )

    def memory_copy(j):
        slot = lax.rem(j, SLOTS)
        return pltpu.make_async_copy(
            memory_hbm.at[:, pl.ds(column(j), BLK)], memory.at[slot], memory_sem.at[slot]
        )

    def fetch(j):
        for i in range(PIECES):
            tokens_copy(j, i).start()
        memory_copy(j).start()

    first = jnp.int32(0)
    for i in range(PIECES):
        grads_copy(i).start()
        tokens_copy(first, i).start()
    memory_copy(first).start()
    for j in range(1, SLOTS - 1):
        fetch(jnp.int32(j))
    warm_copy = pltpu.make_async_copy(warm_hbm, warm_copied, warm_sem)
    warm_copy.start()
    low_rows[...] = jnp.zeros_like(low_rows)
    warm[...] = jnp.zeros_like(warm)

    def on_accumulators(acc0, acc1, part0, part1):
        accs, sums = (acc0, acc1), (part0, part1)

        def multiply(j, begin):
            slot = lax.rem(j, SLOTS)
            for i in range(PIECES):
                if begin:
                    grads_copy(i).wait()
                tokens_copy(j, i).wait()
                for k in range(i * PIECE // MXU, (i + 1) * PIECE // MXU):
                    depth = slice(k * MXU, (k + 1) * MXU)
                    for h in range(2):
                        pltpu.matmul_push_rhs(tokens[slot, depth, h * MXU : (h + 1) * MXU], k % 2, h)
                    left = grads[:, depth]
                    for acc in accs:
                        pltpu.matmul_acc_lhs(acc, left, k % 2)

        def finish(j):
            slot = lax.rem(j, SLOTS)
            memory_copy(j).wait()
            for h, acc in enumerate(accs):
                gradient = pltpu.matmul_pop(acc)
                merged = (gradient + memory[slot, :, h * MXU : (h + 1) * MXU].astype(F32)).astype(BF16)
                merged_ref[:, pl.ds(column(j) + h * MXU, MXU)] = merged
                low_rows[h, 0 : C - MXU, :] = merged[MXU:]

        def sketch_start(j):
            for h, part in enumerate(sums):
                pltpu.matmul_push_rhs(merged_ref[0:MXU, pl.ds(column(j) + h * MXU, MXU)], 0, h)
                pltpu.matmul_push_rhs(low_rows[h], 1, h)
                pltpu.matmul_acc_lhs(part, warm[:, 0:MXU], 0)
                pltpu.matmul_acc_lhs(part, warm[:, MXU:], 1)

        def sketch_end(j):
            at = pl.ds(pl.multiple_of(lax.rem(j, HSTEPS) * LANES, LANES), LANES)
            terms = [pltpu.matmul_pop(part) for part in sums]

            def put(ref):
                for q in range(N_X):
                    term = terms[q // 2][:, q % 2 * LANES : (q % 2 + 1) * LANES].astype(ref.dtype)
                    for p in range(N_Y):
                        ref[q * N_Y + p, :, at] = term[p * ROWS : (p + 1) * ROWS]

            @pl.when(j < HSTEPS)
            def _():
                put(send_ref)

            @pl.when(j >= HSTEPS)
            def _():
                put(own_ref)

        def advance(j):
            @pl.when(j + SLOTS - 1 < STEPS)
            def _():
                fetch(j + SLOTS - 1)

        advance(first)
        multiply(first, True)
        warm_copy.wait()
        warm[:, 0:C] = warm_copied[...]
        finish(first)

        def step(j, carry):
            advance(j)
            multiply(j, False)
            sketch_start(j - 1)
            finish(j)
            sketch_end(j - 1)
            return carry

        lax.fori_loop(1, STEPS, step, 0)
        last = jnp.int32(STEPS - 1)
        sketch_start(last)
        sketch_end(last)

    pl.run_scoped(
        on_accumulators,
        pltpu.ACC(0)((C, MXU), F32),
        pltpu.ACC(1)((C, MXU), F32),
        pltpu.ACC(0)((R, MXU), F32),
        pltpu.ACC(1)((R, MXU), F32),
    )


def merge(core, grads_t, tokens, memory, warm_t):
    vmem, hbm = pl.BlockSpec(memory_space=pltpu.VMEM), pl.BlockSpec(memory_space=pltpu.HBM)
    return pl.pallas_call(
        merge_body,
        out_shape=(
            jax.ShapeDtypeStruct((C, D), BF16),
            jax.ShapeDtypeStruct((PARTS, ROWS, COLS), BF16),
            jax.ShapeDtypeStruct((PARTS, ROWS, COLS), F32),
        ),
        in_specs=[pl.BlockSpec(memory_space=pltpu.SMEM), hbm, hbm, hbm, hbm],
        out_specs=(vmem, vmem, vmem),
        scratch_shapes=[
            pltpu.VMEM((C, TOK), BF16),
            pltpu.VMEM((SLOTS, TOK, BLK), BF16),
            pltpu.VMEM((SLOTS, C, BLK), BF16),
            pltpu.VMEM((2, MXU, MXU), BF16),
            pltpu.VMEM((R, 2 * MXU), BF16),
            pltpu.VMEM((R, C), BF16),
            pltpu.SemaphoreType.DMA((PIECES,)),
            pltpu.SemaphoreType.DMA((SLOTS, PIECES)),
            pltpu.SemaphoreType.DMA((SLOTS,)),
            pltpu.SemaphoreType.DMA(()),
        ],
        compiler_params=pltpu.CompilerParams(vmem_limit_bytes=24 * MIB),
        cost_estimate=pl.CostEstimate(flops=2 * C * D * (TOK + R), bytes_accessed=30_000_000, transcendentals=0),
        name="merge",
    )(core, *(pltpu.with_memory_space_constraint(x, pltpu.HBM) for x in (grads_t, tokens, memory, warm_t)))


def coeff_body(core_ref, own_ref, other_ref, merged_ref, coeff_ref, gram_ref, sketch_hbm, sketch_ref, sketch_sem):
    core = core_ref[0]
    for ref, half in ((own_ref, core), (other_ref, 1 - core)):
        for b in range(HALF // GROUP):
            for q in range(N_X):
                at = pl.ds(pl.multiple_of(half * HALF + b * GROUP + q * LANES, LANES), LANES)
                for p in range(N_Y):
                    sketch_ref[p * ROWS : (p + 1) * ROWS, at] = ref[q * N_Y + p, :, b * LANES : (b + 1) * LANES]
    copy = pltpu.make_async_copy(sketch_ref, sketch_hbm, sketch_sem)
    copy.start()
    sketch = sketch_ref[...]
    gram_ref[...] = lax.dot_general(sketch, sketch, NT, preferred_element_type=F32)
    coeff = lax.dot_general(sketch, merged_ref[...], NT, preferred_element_type=F32)
    each = R // N_DP
    for i in range(N_DP):
        coeff_ref[i, :, 0:C] = coeff[i * each : (i + 1) * each]
        coeff_ref[i, :, C:] = jnp.zeros((each, PAD - C), F32)
    copy.wait()


def coefficients(core, own, other, merged):
    vmem = pl.BlockSpec(memory_space=pltpu.VMEM)
    return pl.pallas_call(
        coeff_body,
        out_shape=(
            jax.ShapeDtypeStruct((N_DP, R // N_DP, PAD), F32),
            jax.ShapeDtypeStruct((R, R), F32),
            pltpu.HBM((R, D), BF16),
        ),
        in_specs=[pl.BlockSpec(memory_space=pltpu.SMEM), vmem, vmem, vmem],
        out_specs=(vmem, vmem, pl.BlockSpec(memory_space=pltpu.HBM)),
        scratch_shapes=[pltpu.VMEM((R, D), BF16), pltpu.SemaphoreType.DMA(())],
        compiler_params=pltpu.CompilerParams(vmem_limit_bytes=8 * MIB),
        cost_estimate=pl.CostEstimate(flops=2 * C * D * R, bytes_accessed=5_000_000, transcendentals=0),
        name="coefficients",
    )(core, own, other, merged)


def basis_body(gram_ref, sketch_hbm, inverse_ref, basis_hbm, sketch_ref, basis_ref, sketch_sem, basis_sem):
    sketch_copy = pltpu.make_async_copy(sketch_hbm, sketch_ref, sketch_sem)
    sketch_copy.start()
    row = lax.broadcasted_iota(jnp.int32, (R, R), 0)
    col = lax.broadcasted_iota(jnp.int32, (R, R), 1)
    state = jnp.concatenate([gram_ref[...], (row == col).astype(F32)], axis=1)
    index = lax.broadcasted_iota(jnp.int32, (R, 1), 0)
    for j in range(R - 1):
        top = (j + 1) // 8 * 8
        lead = state[j : j + 1, :]
        ratio = jnp.where(index[top:] > j, state[top:, j : j + 1] / lead[:, j : j + 1], 0.0)
        tail = state[top:, :] - ratio * lead
        state = tail if top == 0 else jnp.concatenate([state[:top], tail], axis=0)
    diagonal = jnp.sum(jnp.where(row == col, state[:, :R], 0.0), axis=1, keepdims=True)
    inverse = state[:, R:] * lax.rsqrt(diagonal)
    inverse_ref[...] = inverse
    high = inverse.astype(BF16)
    rest = inverse - high.astype(F32)
    middle = rest.astype(BF16)
    low = (rest - middle.astype(F32)).astype(BF16)
    sketch_copy.wait()
    sketch = sketch_ref[...]
    out = jnp.dot(high, sketch, preferred_element_type=F32)
    out += jnp.dot(middle, sketch, preferred_element_type=F32)
    out += jnp.dot(low, sketch, preferred_element_type=F32)
    basis_ref[...] = out.astype(BF16)
    basis_copy = pltpu.make_async_copy(basis_ref, basis_hbm, basis_sem)
    basis_copy.start()
    basis_copy.wait()


def basis(gram, sketch_t):
    vmem, hbm = pl.BlockSpec(memory_space=pltpu.VMEM), pl.BlockSpec(memory_space=pltpu.HBM)
    return pl.pallas_call(
        basis_body,
        out_shape=(jax.ShapeDtypeStruct((R, R), F32), pltpu.HBM((R, D), BF16)),
        in_specs=[vmem, hbm],
        out_specs=(vmem, hbm),
        scratch_shapes=[
            pltpu.VMEM((R, D), BF16),
            pltpu.VMEM((R, D), BF16),
            pltpu.SemaphoreType.DMA(()),
            pltpu.SemaphoreType.DMA(()),
        ],
        compiler_params=pltpu.CompilerParams(vmem_limit_bytes=8 * MIB),
        cost_estimate=pl.CostEstimate(flops=2 * R * R * D * 6, bytes_accessed=20_000_000, transcendentals=0),
        name="basis",
    )(gram, pltpu.with_memory_space_constraint(sketch_t, pltpu.HBM))


def decode_body(
    total_ref, inverse_ref, basis_hbm, merged_ref, update_hbm, error_hbm, start_ref,
    basis, update, error, basis_sem, update_sem, error_sem,
):
    blocks = [pl.ds(j * DBLK, DBLK) for j in range(DSTEPS)]
    arrivals = [
        pltpu.make_async_copy(basis_hbm.at[:, at], basis.at[:, at], basis_sem.at[j]) for j, at in enumerate(blocks)
    ]
    for copy in arrivals:
        copy.start()
    total = jnp.concatenate([total_ref[i, :, 0:C] for i in range(N_DP)], axis=0)
    start = jnp.dot(inverse_ref[...], total, precision=lax.Precision.HIGHEST, preferred_element_type=F32) * (1.0 / N_DP)
    start_ref[...] = start
    half = start.astype(BF16).T
    copies = []
    for j, at in enumerate(blocks):
        arrivals[j].wait()
        decoded = jnp.dot(half, basis[:, at], preferred_element_type=F32)
        update[:, at] = decoded.astype(BF16)
        error[:, at] = (merged_ref[:, at].astype(F32) - decoded).astype(BF16)
        copies.append(pltpu.make_async_copy(update.at[:, at], update_hbm.at[:, at], update_sem.at[j]))
        copies.append(pltpu.make_async_copy(error.at[:, at], error_hbm.at[:, at], error_sem.at[j]))
        copies[-2].start()
        copies[-1].start()
    for copy in copies:
        copy.wait()


DBLK = 512
DSTEPS = D // DBLK


def decode(total, inverse, basis_t, merged):
    vmem, hbm = pl.BlockSpec(memory_space=pltpu.VMEM), pl.BlockSpec(memory_space=pltpu.HBM)
    return pl.pallas_call(
        decode_body,
        out_shape=(
            jax.ShapeDtypeStruct((C, D), BF16),
            jax.ShapeDtypeStruct((C, D), BF16),
            jax.ShapeDtypeStruct((R, C), F32),
        ),
        in_specs=[vmem, vmem, hbm, vmem],
        out_specs=(hbm, hbm, vmem),
        scratch_shapes=[
            pltpu.VMEM((R, D), BF16),
            pltpu.VMEM((C, D), BF16),
            pltpu.VMEM((C, D), BF16),
            pltpu.SemaphoreType.DMA((DSTEPS,)),
            pltpu.SemaphoreType.DMA((DSTEPS,)),
            pltpu.SemaphoreType.DMA((DSTEPS,)),
        ],
        compiler_params=pltpu.CompilerParams(vmem_limit_bytes=16 * MIB),
        cost_estimate=pl.CostEstimate(flops=2 * C * D * R, bytes_accessed=10_500_000, transcendentals=0),
        name="decode",
    )(total, inverse, pltpu.with_memory_space_constraint(basis_t, pltpu.HBM), merged)


def add_up_body(parts_ref, out_ref):
    total = jnp.sum(parts_ref[...].astype(F32), axis=0).astype(out_ref.dtype)
    for i in range(out_ref.shape[0]):
        out_ref[i] = total


def add_up(parts, copies):
    vmem = pl.BlockSpec(memory_space=pltpu.VMEM)
    return pl.pallas_call(
        add_up_body,
        out_shape=jax.ShapeDtypeStruct((copies, *parts.shape[1:]), parts.dtype),
        in_specs=[vmem],
        out_specs=vmem,
        compiler_params=pltpu.CompilerParams(vmem_limit_bytes=4 * MIB),
        cost_estimate=pl.CostEstimate(flops=parts.size, bytes_accessed=2 * parts.size, transcendentals=0),
        name="add_up",
    )(parts)


def per_device(activations, out_grads, error_memory, warm_start):
    core = lax.axis_index("core").astype(jnp.int32).reshape(1)
    swap = [(0, 1), (1, 0)]
    merged, send, own = merge(core, out_grads.T, activations, error_memory[0], warm_start.T)
    mine = (own + lax.ppermute(send, "core", swap).astype(F32)).astype(BF16)
    parts = lax.all_to_all(mine, ("y", "x"), 0, 0, tiled=True)
    parts = lax.all_to_all(add_up(parts, N_Z), "z", 0, 0, tiled=True)
    sketch_own = lax.all_to_all(add_up(parts, PARTS), ("y", "x"), 0, 0, tiled=True)
    sketch_other = lax.ppermute(sketch_own, "core", swap)
    coeff, gram, sketch_t = coefficients(core, sketch_own, sketch_other, merged)
    terms = lax.all_to_all(coeff, ("y", "z"), 0, 0, tiled=True)
    total = lax.all_to_all(add_up(terms, N_DP), ("y", "z"), 0, 0, tiled=True)
    inverse, basis_t = basis(gram, sketch_t)
    update, new_error, start_t = decode(total, inverse, basis_t, merged)
    return update, new_error[None], start_t.T


def solution(mesh):
    fine = Mesh(mesh.devices.reshape(N_Y, N_Z, N_X, 2), ("y", "z", "x", "core"))
    d, t = ("y", "z"), ("x", "core")
    return jax.shard_map(
        per_device,
        mesh=fine,
        in_specs=(P(d, None), P(d, t), P(d, t, None), P(t, None)),
        out_specs=(P(t, None), P(d, t, None), P(t, None)),
        check_vma=False,
    )
```

time: 459 us -> 98.5 us (0.21)
  waiting for transfers between devices: 401 us -> 6.49 us
  blocking collectives: 0 us -> 58.6 us
  Pallas kernels: 0 us -> 28.4 us
  matrix products: 27.2 us -> 0 us
  between operations: 14.1 us -> 0.69 us
  other arithmetic: 13 us -> 0.08 us
    psum x2 -> x0, waiting for transfers between devices: 401 us -> none  [the longest x1 262 us: per_device(): sketch = lax.psum(sketch_local, ('dp', 'tensor'))]
    all_to_all x0 -> x4, blocking collectives: none -> 58.6 us  [the longest x1 17.7 us: per_device(): parts = lax.all_to_all(add_up(parts, N_Z), 'z', 0, 0, tiled=True)]
    pallas_call x0 -> x7, Pallas kernels: none -> 28.4 us  [the longest x1 13.7 us: merge(): pl.pallas_call(merge_body, out_shape=(jax.ShapeDtypeStruct((C, D), BF16),...]
    dot_general x5 -> x0, matrix products: 25.9 us -> none  [the longest x1 11.6 us: per_device(): lax.dot_general(out_grads, activations, CONTRACT_ROWS, preferred_element_...]
    another operation x5 -> x0, other arithmetic: 12.1 us -> none  [the longest x3 6.52 us: orthonormal(): factor = jnp.linalg.cholesky(gram_total)]
  transfers between devices with their start and end apart: 2 -> 3, of which waited for: 2 -> 3; matrix products, arithmetic and copies ran while one was open for 0% -> 0% of each run, Pallas kernels for 0% -> 7%
where the time goes in v1:
time: 98.5 us; the launch traced here: 98.2 us
  blocking collectives  58.6 us (59%)
  Pallas kernels  28.4 us (29%)
  waiting for transfers between devices  6.49 us (7%)
  starting transfers between devices  3.95 us (4%)
    all_to_all x1, blocking collectives, per_device(): parts = lax.all_to_all(add_up(parts, N_Z), 'z', 0, 0, tiled=True)  17.7 us
    all_to_all x1, blocking collectives, per_device(): parts = lax.all_to_all(mine, ('y', 'x'), 0, 0, tiled=True)  15.6 us
    pallas_call x1, Pallas kernels, merge(): pl.pallas_call(merge_body, out_shape=(jax.ShapeDtypeStruct((C, D), BF16),...  13.7 us
    all_to_all x1, blocking collectives, per_device(): terms = lax.all_to_all(coeff, ('y', 'z'), 0, 0, tiled=True)  13.4 us
    all_to_all x1, blocking collectives, per_device(): lax.all_to_all(add_up(parts, PARTS), ('y', 'x'), 0, 0, tiled=True)  11.9 us
    pallas_call x1, Pallas kernels, basis(): pl.pallas_call(basis_body, out_shape=(jax.ShapeDtypeStruct((R, R), F32),...  7.02 us
    pallas_call x1, Pallas kernels, decode(): pl.pallas_call(decode_body, out_shape=(jax.ShapeDtypeStruct((C, D), BF16)...  4.84 us
    all_to_all x1, starting transfers between devices, per_device(): total = lax.all_to_all(add_up(terms, N_DP), ('y', 'z'), 0, 0, tiled=True)  3.86 us
  transfers between devices with their start and end apart: 3, of which 3 were waited for; matrix products, arithmetic and copies ran while one was open for 0% of the time, Pallas kernels for 7%

profile of v1, /device:TPU:2, one launch (start us, length us, event | category | flops | bytes accessed | tf_op | source)
XLA Modules:
  0.0 98.2 jit_solution(11170867254223247152)
XLA Ops:
  0.6 13.7 %merge.1 = (bf16[320,5120]{1,0:T(8,128)(2,1)S(1)}, bf16[16,16,640]{2,1,0:T(8,128)(2,1)S(1)}, f32[16,16,640]{2,1,0:T(8,128)S(1)}) custom-call(s32[1]{0:T(128)} %bitcast.core_ref, bf16[320,2048]{1,0:T(8,128)(2,1)} %bitcast.8, bf16[2048,5120]{1,0:T(8,128)(2,1)} %tokens_hbm.1, bf16[320,5120]{1,0:T(8,128)(2,1)} %bitcast.6, bf16[64,320]{1,0:T(8,128)(2,1)} %bitcast.10), custom_call_target="tpu_custom_call" | custom-call | flops 6920601600 | bytes 30000000 | tf_op jit(solution)/shard_map/merge/pallas_call | solution.py:163
  14.4 0.1 collective-permute-start
  14.5 1.6 %collective-permute-done = bf16[16,16,640]{2,1,0:T(8,128)(2,1)S(1)} collective-permute-done((bf16[16,16,640]{2,1,0:T(8,128)(2,1)S(1)}, bf16[16,16,640]{2,1,0:T(8,128)(2,1)S(1)}, u32[]{:S(2)}, u32[]{:S(2)}) %collective-permute-start) | collective-permute-done | bytes 327712 | tf_op jit(solution)/shard_map/ppermute | solution.py:358
  16.1 0.1 add_convert_fusion
  16.2 15.6 %all_to_all.25.parts_ref = bf16[16,16,640]{2,1,0:T(8,128)(2,1)S(1)} all-to-all(bf16[16,16,640]{2,1,0:T(8,128)(2,1)S(1)} %add_convert_fusion), channel_id=1, replica_groups=mesh['y'=4,'z'=8,'x'=4,'core'=2] {'y','x'}, dimensions={0} | all-to-all | bytes 655360 | tf_op jit(solution)/shard_map/all_to_all | solution.py:359
  31.8 0.1 add_up.3
  31.8 17.7 %all_to_all.26.parts_ref = bf16[8,16,640]{2,1,0:T(8,128)(2,1)S(1)} all-to-all(bf16[8,16,640]{2,1,0:T(8,128)(2,1)S(1)} %add_up.3), channel_id=1, replica_groups=mesh['y'=4,'z'=8,'x'=4,'core'=2] {'z'}, dimensions={0} | all-to-all | bytes 327680 | tf_op jit(solution)/shard_map/all_to_all | solution.py:360
  49.5 11.9 %all_to_all.27.own_ref = bf16[16,16,640]{2,1,0:T(8,128)(2,1)S(1)} all-to-all(bf16[16,16,640]{2,1,0:T(8,128)(2,1)S(1)} %add_up.4), channel_id=1, replica_groups=mesh['y'=4,'z'=8,'x'=4,'core'=2] {'y','x'}, dimensions={0} | all-to-all | bytes 655360 | tf_op jit(solution)/shard_map/all_to_all | solution.py:361
  61.5 0.0 collective-permute-start.1
  61.5 1.6 %collective-permute-done.1.other_ref = bf16[16,16,640]{2,1,0:T(8,128)(2,1)S(1)} collective-permute-done((bf16[16,16,640]{2,1,0:T(8,128)(2,1)S(1)}, bf16[16,16,640]{2,1,0:T(8,128)(2,1)S(1)}, u32[]{:S(2)}, u32[]{:S(2)}) %collective-permute-start.1) | collective-permute-done | bytes 327712 | tf_op jit(solution)/shard_map/ppermute | solution.py:362
  63.1 2.0 %coefficients.1 = (f32[32,2,384]{2,1,0:T(2,128)S(1)}, f32[64,64]{1,0:T(8,128)S(1)}, bf16[64,5120]{1,0:T(8,128)(2,1)}) custom-call(s32[1]{0:T(128)} %bitcast.core_ref, bf16[16,16,640]{2,1,0:T(8,128)(2,1)S(1)} %all_to_all.27.own_ref, bf16[16,16,640]{2,1,0:T(8,128)(2,1)S(1)} %collective-permute-done.1.other_ref, bf16[320,5120]{1,0:T(8,128)(2,1)S(1)} %get-tuple-element.16.merged_ref), custom_call_target="tpu_custom_call" | custom-call | flops 209715200 | bytes 5000000 | tf_op jit(solution)/shard_map/coefficients/pallas_call | solution.py:212
  65.1 13.4 %all_to_all.28.parts_ref = f32[32,2,384]{2,1,0:T(2,128)S(1)} all-to-all(f32[32,2,384]{2,1,0:T(2,128)S(1)} %get-tuple-element.17), channel_id=1, replica_groups=mesh['y'=4,'z'=8,'x'=4,'core'=2] {'y','z'}, dimensions={0} | all-to-all | bytes 196608 | tf_op jit(solution)/shard_map/all_to_all | solution.py:364
  78.5 0.7 add_up.5
  79.2 3.9 %all-to-all-start.4 = ((f32[32,2,384]{2,1,0:T(2,128)}), f32[32,2,384]{2,1,0:T(2,128)S(1)}, u32[]{:S(2)}, u32[]{:S(2)}) async-start(f32[32,2,384]{2,1,0:T(2,128)} %add_up.5), calls=%async_computation.4 | async-start | bytes 196608 | tf_op jit(solution)/shard_map/all_to_all | solution.py:365
  83.1 7.0 %basis.1 = (f32[64,64]{1,0:T(8,128)S(1)}, bf16[64,5120]{1,0:T(8,128)(2,1)}) custom-call(f32[64,64]{1,0:T(8,128)S(1)} %get-tuple-element.18.gram_ref, bf16[64,5120]{1,0:T(8,128)(2,1)} %get-tuple-element.19.sketch_hbm), custom_call_target="tpu_custom_call" | custom-call | flops 251658240 | bytes 20000000 | tf_op jit(solution)/shard_map/basis/pallas_call | solution.py:261
  90.1 3.2 %all-to-all-done.4.total_ref = f32[32,2,384]{2,1,0:T(2,128)S(1)} async-done(((f32[32,2,384]{2,1,0:T(2,128)}), f32[32,2,384]{2,1,0:T(2,128)S(1)}, u32[]{:S(2)}, u32[]{:S(2)}) %all-to-all-start.4) | async-done | bytes 98336 | tf_op jit(solution)/shard_map/all_to_all | solution.py:365
  93.3 4.8 %decode.1 = (bf16[320,5120]{1,0:T(8,128)(2,1)}, bf16[320,5120]{1,0:T(8,128)(2,1)}, f32[64,320]{1,0:T(8,128)}) custom-call(f32[32,2,384]{2,1,0:T(2,128)S(1)} %all-to-all-done.4.total_ref, f32[64,64]{1,0:T(8,128)S(1)} %get-tuple-element.20.inverse_ref, bf16[64,5120]{1,0:T(8,128)(2,1)} %get-tuple-element.21.basis_hbm, ...), custom_call_target="tpu_custom_call" | custom-call | flops 209715200 | bytes 10500000 | tf_op jit(solution)/shard_map/decode/pallas_call | solution.py:312
  (1 shorter events, 0.0 us)
Async XLA Ops:
  14.4 1.7 %collective-permute-start = (bf16[16,16,640]{2,1,0:T(8,128)(2,1)S(1)}, bf16[16,16,640]{2,1,0:T(8,128)(2,1)S(1)}, u32[]{:S(2)}, u32[]{:S(2)}) collective-permute-start(bf16[16,16,640]{2,1,0:T(8,128)(2,1)S(1)} %get-tuple-element.15), channel_id=1, source_target_pairs={{0,1},{1,0},{2,3},{3,2},{4,5},{5,4},{6,7},{7,6},{8,9},{9,8},{10,11... | collective-permute-start | bytes 983048 | tf_op jit(solution)/shard_map/ppermute | solution.py:358
  61.5 1.6 %collective-permute-start.1 = (bf16[16,16,640]{2,1,0:T(8,128)(2,1)S(1)}, bf16[16,16,640]{2,1,0:T(8,128)(2,1)S(1)}, u32[]{:S(2)}, u32[]{:S(2)}) collective-permute-start(bf16[16,16,640]{2,1,0:T(8,128)(2,1)S(1)} %all_to_all.27.own_ref), channel_id=1, source_target_pairs={{0,1},{1,0},{2,3},{3,2},{4,5},{5,4},{6,7},{7,6},{8,9},{9,8},{10,11... | collective-permute-start | bytes 983048 | tf_op jit(solution)/shard_map/ppermute | solution.py:362
  79.2 14.1 %all-to-all-start.4 = ((f32[32,2,384]{2,1,0:T(2,128)}), f32[32,2,384]{2,1,0:T(2,128)S(1)}, u32[]{:S(2)}, u32[]{:S(2)}) async-start(f32[32,2,384]{2,1,0:T(2,128)} %add_up.5), calls=%async_computation.4 | async-start | bytes 196608 | tf_op jit(solution)/shard_map/all_to_all | solution.py:365

commit v2 on v1

v2 whole, which is shorter than its diff:
```python
import jax
import jax.numpy as jnp
from jax import lax
from jax.experimental import pallas as pl
from jax.experimental.pallas import tpu as pltpu
from jax.sharding import Mesh, PartitionSpec as P

D = 5120
C = 320
R = 64
TOK = 2048
N_DP = 32
N_X, N_Y, N_Z = 4, 4, 8
HALF = D // 2
BLK = 512
MXU = 256
SLOTS = 3
LANES = 128
GROUP = N_X * LANES
STEPS = D // BLK
KEPT = 6
WIDE = KEPT * BLK
HSTEPS = STEPS // 2
ROWS = R // N_Y
COLS = HALF // N_X
PARTS = N_X * N_Y
PAD = 384
F32, BF16 = jnp.float32, jnp.bfloat16
NT = (((1,), (1,)), ((), ()))
TN = (((0,), (0,)), ((), ()))
MIB = 1024 * 1024


def merge_body(
    core_ref, grads_hbm, tokens_hbm, memory_hbm, warm_hbm, kept_ref, rest_ref, rest_hbm, send_ref, own_ref,
    grads, tokens, memory, high_rows, low_rows, warm, warm_copied, grads_sem, tokens_sem, memory_sem, warm_sem, rest_sem,
):
    core = core_ref[0]

    def block(j):
        half = jnp.where(j < HSTEPS, 1 - core, core)
        return half * HSTEPS + lax.rem(j + half * (KEPT - HSTEPS), HSTEPS)

    def column(j):
        return pl.multiple_of(block(j) * BLK, BLK)

    def spill(j):
        at = pl.ds(pl.multiple_of((block(j) - KEPT) * BLK, BLK), BLK)
        return pltpu.make_async_copy(rest_ref.at[:, at], rest_hbm.at[:, at], rest_sem.at[block(j) - KEPT])

    grads_copy = pltpu.make_async_copy(grads_hbm, grads, grads_sem)

    def copies(j):
        slot, at = lax.rem(j, SLOTS), pl.ds(column(j), BLK)
        return (
            pltpu.make_async_copy(tokens_hbm.at[:, at], tokens.at[slot], tokens_sem.at[slot]),
            pltpu.make_async_copy(memory_hbm.at[:, at], memory.at[slot], memory_sem.at[slot]),
        )

    def fetch(j):
        for copy in copies(j):
            copy.start()

    def arrive(j):
        for copy in copies(j):
            copy.wait()

    first = jnp.int32(0)
    grads_copy.start()
    fetch(first)
    warm_copy = pltpu.make_async_copy(warm_hbm, warm_copied, warm_sem)
    warm_copy.start()
    low_rows[...] = jnp.zeros_like(low_rows)
    warm[...] = jnp.zeros_like(warm)

    def on_accumulators(acc0, acc1, part0, part1):
        accs, sums = (acc0, acc1), (part0, part1)

        def multiply(j):
            slot = lax.rem(j, SLOTS)
            for k in range(TOK // MXU):
                depth = slice(k * MXU, (k + 1) * MXU)
                for h in range(2):
                    pltpu.matmul_push_rhs(tokens[slot, depth, h * MXU : (h + 1) * MXU], k % 2, h)
                left = grads[:, depth]
                for acc in accs:
                    pltpu.matmul_acc_lhs(acc, left, k % 2)

        def finish(j):
            slot = lax.rem(j, SLOTS)
            for h, acc in enumerate(accs):
                gradient = pltpu.matmul_pop(acc)
                merged = (gradient + memory[slot, :, h * MXU : (h + 1) * MXU].astype(F32)).astype(BF16)
                high_rows[h] = merged[0:MXU]
                low_rows[h, 0 : C - MXU, :] = merged[MXU:]

                @pl.when(block(j) < KEPT)
                def _():
                    kept_ref[:, pl.ds(column(j) + h * MXU, MXU)] = merged

                @pl.when(block(j) >= KEPT)
                def _():
                    rest_ref[:, pl.ds(column(j) - WIDE + h * MXU, MXU)] = merged

            @pl.when(block(j) >= KEPT)
            def _():
                spill(j).start()

        def sketch_start(j):
            for h, part in enumerate(sums):
                pltpu.matmul_push_rhs(high_rows[h], 0, h)
                pltpu.matmul_push_rhs(low_rows[h], 1, h)
                pltpu.matmul_acc_lhs(part, warm[:, 0:MXU], 0)
                pltpu.matmul_acc_lhs(part, warm[:, MXU:], 1)

        def sketch_end(j):
            at = pl.ds(pl.multiple_of(lax.rem(block(j), HSTEPS) * LANES, LANES), LANES)
            terms = [pltpu.matmul_pop(part) for part in sums]

            def put(ref):
                for q in range(N_X):
                    term = terms[q // 2][:, q % 2 * LANES : (q % 2 + 1) * LANES].astype(ref.dtype)
                    for p in range(N_Y):
                        ref[q * N_Y + p, :, at] = term[p * ROWS : (p + 1) * ROWS]

            @pl.when(j < HSTEPS)
            def _():
                put(send_ref)

            @pl.when(j >= HSTEPS)
            def _():
                put(own_ref)

        grads_copy.wait()
        fetch(first + 1)
        arrive(first)
        for j in range(2, SLOTS):
            fetch(jnp.int32(j))
        multiply(first)
        warm_copy.wait()
        warm[:, 0:C] = warm_copied[...]
        finish(first)

        def step(j, carry):
            arrive(j)

            @pl.when(j + SLOTS - 1 < STEPS)
            def _():
                fetch(j + SLOTS - 1)

            multiply(j)
            sketch_start(j - 1)
            finish(j)
            sketch_end(j - 1)
            return carry

        lax.fori_loop(1, STEPS, step, 0)
        last = jnp.int32(STEPS - 1)
        sketch_start(last)
        sketch_end(last)
        for i in range(STEPS - KEPT):
            at = pl.ds(i * BLK, BLK)
            pltpu.make_async_copy(rest_ref.at[:, at], rest_hbm.at[:, at], rest_sem.at[i]).wait()

    pl.run_scoped(
        on_accumulators,
        pltpu.ACC(0)((C, MXU), F32),
        pltpu.ACC(1)((C, MXU), F32),
        pltpu.ACC(0)((R, MXU), F32),
        pltpu.ACC(1)((R, MXU), F32),
    )


def merge(core, grads_t, tokens, memory, warm_t):
    vmem, hbm = pl.BlockSpec(memory_space=pltpu.VMEM), pl.BlockSpec(memory_space=pltpu.HBM)
    return pl.pallas_call(
        merge_body,
        out_shape=(
            jax.ShapeDtypeStruct((C, WIDE), BF16),
            jax.ShapeDtypeStruct((C, D - WIDE), BF16),
            pltpu.HBM((C, D - WIDE), BF16),
            jax.ShapeDtypeStruct((PARTS, ROWS, COLS), BF16),
            jax.ShapeDtypeStruct((PARTS, ROWS, COLS), F32),
        ),
        in_specs=[pl.BlockSpec(memory_space=pltpu.SMEM), hbm, hbm, hbm, hbm],
        out_specs=(vmem, vmem, hbm, vmem, vmem),
        scratch_shapes=[
            pltpu.VMEM((C, TOK), BF16),
            pltpu.VMEM((SLOTS, TOK, BLK), BF16),
            pltpu.VMEM((SLOTS, C, BLK), BF16),
            pltpu.VMEM((2, MXU, MXU), BF16),
            pltpu.VMEM((2, MXU, MXU), BF16),
            pltpu.VMEM((R, 2 * MXU), BF16),
            pltpu.VMEM((R, C), BF16),
            pltpu.SemaphoreType.DMA(()),
            pltpu.SemaphoreType.DMA((SLOTS,)),
            pltpu.SemaphoreType.DMA((SLOTS,)),
            pltpu.SemaphoreType.DMA(()),
            pltpu.SemaphoreType.DMA((STEPS - KEPT,)),
        ],
        compiler_params=pltpu.CompilerParams(vmem_limit_bytes=24 * MIB),
        cost_estimate=pl.CostEstimate(flops=2 * C * D * (TOK + R), bytes_accessed=30_000_000, transcendentals=0),
        name="merge",
    )(core, *(pltpu.with_memory_space_constraint(x, pltpu.HBM) for x in (grads_t, tokens, memory, warm_t)))


def coeff_body(core_ref, own_ref, other_ref, kept_ref, rest_ref, coeff_ref, gram_ref, sketch_ref):
    core = core_ref[0]
    for ref, half in ((own_ref, core), (other_ref, 1 - core)):
        for b in range(HALF // GROUP):
            for q in range(N_X):
                at = pl.ds(pl.multiple_of(half * HALF + b * GROUP + q * LANES, LANES), LANES)
                for p in range(N_Y):
                    sketch_ref[p * ROWS : (p + 1) * ROWS, at] = ref[q * N_Y + p, :, b * LANES : (b + 1) * LANES]
    sketch = sketch_ref[...]
    gram_ref[...] = lax.dot_general(sketch, sketch, NT, preferred_element_type=F32)
    coeff = lax.dot_general(sketch[:, :WIDE], kept_ref[...], NT, preferred_element_type=F32)
    coeff += lax.dot_general(sketch[:, WIDE:], rest_ref[...], NT, preferred_element_type=F32)
    each = R // N_DP
    for i in range(N_DP):
        coeff_ref[i, :, 0:C] = coeff[i * each : (i + 1) * each]
        coeff_ref[i, :, C:] = jnp.zeros((each, PAD - C), F32)


def coefficients(core, own, other, kept, rest):
    vmem = pl.BlockSpec(memory_space=pltpu.VMEM)
    return pl.pallas_call(
        coeff_body,
        out_shape=(
            jax.ShapeDtypeStruct((N_DP, R // N_DP, PAD), F32),
            jax.ShapeDtypeStruct((R, R), F32),
            jax.ShapeDtypeStruct((R, D), BF16),
        ),
        in_specs=[pl.BlockSpec(memory_space=pltpu.SMEM), vmem, vmem, vmem, vmem],
        out_specs=(vmem, vmem, vmem),
        compiler_params=pltpu.CompilerParams(vmem_limit_bytes=8 * MIB),
        cost_estimate=pl.CostEstimate(flops=2 * C * D * R, bytes_accessed=5_000_000, transcendentals=0),
        name="coefficients",
    )(core, own, other, kept, rest)


def basis_body(gram_ref, sketch_ref, inverse_ref, basis_ref):
    row = lax.broadcasted_iota(jnp.int32, (R, R), 0)
    col = lax.broadcasted_iota(jnp.int32, (R, R), 1)
    state = jnp.concatenate([gram_ref[...], (row == col).astype(F32)], axis=1)
    index = lax.broadcasted_iota(jnp.int32, (R, 1), 0)
    for j in range(R - 1):
        top = (j + 1) // 8 * 8
        lead = state[j : j + 1, :]
        ratio = jnp.where(index[top:] > j, state[top:, j : j + 1] / lead[:, j : j + 1], 0.0)
        tail = state[top:, :] - ratio * lead
        state = tail if top == 0 else jnp.concatenate([state[:top], tail], axis=0)
    diagonal = jnp.sum(jnp.where(row == col, state[:, :R], 0.0), axis=1, keepdims=True)
    inverse = state[:, R:] * lax.rsqrt(diagonal)
    inverse_ref[...] = inverse
    high = inverse.astype(BF16)
    rest = inverse - high.astype(F32)
    middle = rest.astype(BF16)
    low = (rest - middle.astype(F32)).astype(BF16)
    sketch = sketch_ref[...]
    out = jnp.dot(high, sketch, preferred_element_type=F32)
    out += jnp.dot(middle, sketch, preferred_element_type=F32)
    out += jnp.dot(low, sketch, preferred_element_type=F32)
    basis_ref[...] = out.astype(BF16)


def basis(gram, sketch_t):
    vmem = pl.BlockSpec(memory_space=pltpu.VMEM)
    return pl.pallas_call(
        basis_body,
        out_shape=(jax.ShapeDtypeStruct((R, R), F32), jax.ShapeDtypeStruct((R, D), BF16)),
        in_specs=[vmem, vmem],
        out_specs=(vmem, vmem),
        compiler_params=pltpu.CompilerParams(vmem_limit_bytes=8 * MIB),
        cost_estimate=pl.CostEstimate(flops=2 * R * R * D * 6, bytes_accessed=20_000_000, transcendentals=0),
        name="basis",
    )(gram, sketch_t)


def decode_body(
    total_ref, inverse_ref, basis_ref, kept_ref, rest_hbm, update_hbm, error_hbm, start_ref,
    rest, update, error, rest_sem, update_sem, error_sem,
):
    rest_copy = pltpu.make_async_copy(rest_hbm, rest, rest_sem)
    rest_copy.start()
    total = jnp.concatenate([total_ref[i, :, 0:C] for i in range(N_DP)], axis=0)
    start = jnp.dot(inverse_ref[...], total, precision=lax.Precision.HIGHEST, preferred_element_type=F32) * (1.0 / N_DP)
    start_ref[...] = start
    half = start.astype(BF16).T
    copies = []
    for j in range(DSTEPS):
        at = pl.ds(j * DBLK, DBLK)
        if j * DBLK == WIDE:
            rest_copy.wait()
        merged = kept_ref[:, at] if j * DBLK < WIDE else rest[:, j * DBLK - WIDE : (j + 1) * DBLK - WIDE]
        decoded = jnp.dot(half, basis_ref[:, at], preferred_element_type=F32)
        update[:, at] = decoded.astype(BF16)
        error[:, at] = (merged.astype(F32) - decoded).astype(BF16)
        copies.append(pltpu.make_async_copy(update.at[:, at], update_hbm.at[:, at], update_sem.at[j]))
        copies.append(pltpu.make_async_copy(error.at[:, at], error_hbm.at[:, at], error_sem.at[j]))
        copies[-2].start()
        copies[-1].start()
    for copy in copies:
        copy.wait()


DBLK = 1024
DSTEPS = D // DBLK


def decode(total, inverse, basis_t, kept, rest):
    vmem, hbm = pl.BlockSpec(memory_space=pltpu.VMEM), pl.BlockSpec(memory_space=pltpu.HBM)
    return pl.pallas_call(
        decode_body,
        out_shape=(
            jax.ShapeDtypeStruct((C, D), BF16),
            jax.ShapeDtypeStruct((C, D), BF16),
            jax.ShapeDtypeStruct((R, C), F32),
        ),
        in_specs=[vmem, vmem, vmem, vmem, hbm],
        out_specs=(hbm, hbm, vmem),
        scratch_shapes=[
            pltpu.VMEM((C, D - WIDE), BF16),
            pltpu.VMEM((C, D), BF16),
            pltpu.VMEM((C, D), BF16),
            pltpu.SemaphoreType.DMA(()),
            pltpu.SemaphoreType.DMA((DSTEPS,)),
            pltpu.SemaphoreType.DMA((DSTEPS,)),
        ],
        compiler_params=pltpu.CompilerParams(vmem_limit_bytes=16 * MIB),
        cost_estimate=pl.CostEstimate(flops=2 * C * D * R, bytes_accessed=10_500_000, transcendentals=0),
        name="decode",
    )(total, inverse, basis_t, kept, pltpu.with_memory_space_constraint(rest, pltpu.HBM))


def add_up_body(parts_ref, out_ref):
    total = jnp.sum(parts_ref[...].astype(F32), axis=0).astype(out_ref.dtype)
    for i in range(out_ref.shape[0]):
        out_ref[i] = total


def add_up(parts, copies):
    vmem = pl.BlockSpec(memory_space=pltpu.VMEM)
    return pl.pallas_call(
        add_up_body,
        out_shape=jax.ShapeDtypeStruct((copies, *parts.shape[1:]), parts.dtype),
        in_specs=[vmem],
        out_specs=vmem,
        compiler_params=pltpu.CompilerParams(vmem_limit_bytes=4 * MIB),
        cost_estimate=pl.CostEstimate(flops=parts.size, bytes_accessed=2 * parts.size, transcendentals=0),
        name="add_up",
    )(parts)


def per_device(activations, out_grads, error_memory, warm_start):
    core = lax.axis_index("core").astype(jnp.int32).reshape(1)
    swap = [(0, 1), (1, 0)]
    kept, rest, rest_hbm, send, own = merge(core, out_grads.T, activations, error_memory[0], warm_start.T)
    mine = (own + lax.ppermute(send, "core", swap).astype(F32)).astype(BF16)
    parts = lax.all_to_all(mine, ("y", "x"), 0, 0, tiled=True)
    parts = lax.all_to_all(add_up(parts, N_Z), "z", 0, 0, tiled=True)
    sketch_own = lax.all_to_all(add_up(parts, PARTS), ("y", "x"), 0, 0, tiled=True)
    sketch_other = lax.ppermute(sketch_own, "core", swap)
    coeff, gram, sketch_t = coefficients(core, sketch_own, sketch_other, kept, rest)
    terms = lax.all_to_all(coeff, ("y", "z"), 0, 0, tiled=True)
    total = lax.all_to_all(add_up(terms, N_DP), ("y", "z"), 0, 0, tiled=True)
    inverse, basis_t = basis(gram, sketch_t)
    update, new_error, start_t = decode(total, inverse, basis_t, kept, rest_hbm)
    return update, new_error[None], start_t.T


def solution(mesh):
    fine = Mesh(mesh.devices.reshape(N_Y, N_Z, N_X, 2), ("y", "z", "x", "core"))
    d, t = ("y", "z"), ("x", "core")
    return jax.shard_map(
        per_device,
        mesh=fine,
        in_specs=(P(d, None), P(d, t), P(d, t, None), P(t, None)),
        out_specs=(P(t, None), P(d, t, None), P(t, None)),
        check_vma=False,
    )
```

time: 98.5 us -> 95.6 us (0.971)
  Pallas kernels: 28.4 us -> 24.6 us
    pallas_call x1, Pallas kernels: 13.7 us -> 12.2 us  [merge(): pl.pallas_call(merge_body, out_shape=(jax.ShapeDtypeStruct((C, WIDE), BF1...]
  transfers between devices with their start and end apart: 3 -> 3, of which waited for: 3 -> 3; matrix products, arithmetic and copies ran while one was open for 0% -> 0% of each run, Pallas kernels for 7% -> 6%
where the time goes in v2:
time: 95.6 us; the launch traced here: 95.2 us
  blocking collectives  58.5 us (61%)
  Pallas kernels  24.6 us (26%)
  waiting for transfers between devices  7.43 us (8%)
  starting transfers between devices  3.95 us (4%)
    all_to_all x1, blocking collectives, per_device(): parts = lax.all_to_all(add_up(parts, N_Z), 'z', 0, 0, tiled=True)  17.7 us
    all_to_all x1, blocking collectives, per_device(): parts = lax.all_to_all(mine, ('y', 'x'), 0, 0, tiled=True)  15.6 us
    all_to_all x1, blocking collectives, per_device(): terms = lax.all_to_all(coeff, ('y', 'z'), 0, 0, tiled=True)  13.4 us
    pallas_call x1, Pallas kernels, merge(): pl.pallas_call(merge_body, out_shape=(jax.ShapeDtypeStruct((C, WIDE), BF1...  12.2 us
    all_to_all x1, blocking collectives, per_device(): lax.all_to_all(add_up(parts, PARTS), ('y', 'x'), 0, 0, tiled=True)  11.9 us
    pallas_call x1, Pallas kernels, basis(): pl.pallas_call(basis_body, out_shape=(jax.ShapeDtypeStruct((R, R), F32),...  6.08 us
    all_to_all x1, waiting for transfers between devices, per_device(): total = lax.all_to_all(add_up(terms, N_DP), ('y', 'z'), 0, 0, tiled=True)  4.18 us
    pallas_call x1, Pallas kernels, decode(): pl.pallas_call(decode_body, out_shape=(jax.ShapeDtypeStruct((C, D), BF16)...  4.12 us
  transfers between devices with their start and end apart: 3, of which 3 were waited for; matrix products, arithmetic and copies ran while one was open for 0% of the time, Pallas kernels for 6%

profile of v2, /device:TPU:2, one launch (start us, length us, event | category | flops | bytes accessed | tf_op | source)
XLA Modules:
  0.0 95.2 jit_solution(13654227981416021055)
XLA Ops:
  0.6 12.2 %merge.1 = (bf16[320,3072]{1,0:T(8,128)(2,1)S(1)}, bf16[320,2048]{1,0:T(8,128)(2,1)S(1)}, bf16[320,2048]{1,0:T(8,128)(2,1)}, bf16[16,16,640]{2,1,0:T(8,128)(2,1)S(1)}, f32[16,16,640]{2,1,0:T(8,128)S(1)}) custom-call(s32[1]{0:T(128)} %bitcast.core_ref, bf16[320,2048]{1,0:T(8,128)(2,1)} %bitcast.8, bf16[2048,5120]{1,0:T(8,128)(2,1)} %tokens_hbm.1, ...), custom_call_target="tpu_custom_call" | custom-call | flops 6920601600 | bytes 30000000 | tf_op jit(solution)/shard_map/merge/pallas_call | solution.py:176
  12.9 0.1 collective-permute-start
  13.0 1.6 %collective-permute-done = bf16[16,16,640]{2,1,0:T(8,128)(2,1)S(1)} collective-permute-done((bf16[16,16,640]{2,1,0:T(8,128)(2,1)S(1)}, bf16[16,16,640]{2,1,0:T(8,128)(2,1)S(1)}, u32[]{:S(2)}, u32[]{:S(2)}) %collective-permute-start) | collective-permute-done | bytes 327712 | tf_op jit(solution)/shard_map/ppermute | solution.py:359
  14.6 0.1 add_convert_fusion
  14.7 15.6 %all_to_all.25.parts_ref = bf16[16,16,640]{2,1,0:T(8,128)(2,1)S(1)} all-to-all(bf16[16,16,640]{2,1,0:T(8,128)(2,1)S(1)} %add_convert_fusion), channel_id=1, replica_groups=mesh['y'=4,'z'=8,'x'=4,'core'=2] {'y','x'}, dimensions={0} | all-to-all | bytes 655360 | tf_op jit(solution)/shard_map/all_to_all | solution.py:360
  30.3 0.1 add_up.3
  30.3 17.7 %all_to_all.26.parts_ref = bf16[8,16,640]{2,1,0:T(8,128)(2,1)S(1)} all-to-all(bf16[8,16,640]{2,1,0:T(8,128)(2,1)S(1)} %add_up.3), channel_id=1, replica_groups=mesh['y'=4,'z'=8,'x'=4,'core'=2] {'z'}, dimensions={0} | all-to-all | bytes 327680 | tf_op jit(solution)/shard_map/all_to_all | solution.py:361
  48.0 11.9 %all_to_all.27.own_ref = bf16[16,16,640]{2,1,0:T(8,128)(2,1)S(1)} all-to-all(bf16[16,16,640]{2,1,0:T(8,128)(2,1)S(1)} %add_up.4), channel_id=1, replica_groups=mesh['y'=4,'z'=8,'x'=4,'core'=2] {'y','x'}, dimensions={0} | all-to-all | bytes 655360 | tf_op jit(solution)/shard_map/all_to_all | solution.py:362
  60.0 0.0 collective-permute-start.1
  60.0 1.6 %collective-permute-done.1.other_ref = bf16[16,16,640]{2,1,0:T(8,128)(2,1)S(1)} collective-permute-done((bf16[16,16,640]{2,1,0:T(8,128)(2,1)S(1)}, bf16[16,16,640]{2,1,0:T(8,128)(2,1)S(1)}, u32[]{:S(2)}, u32[]{:S(2)}) %collective-permute-start.1) | collective-permute-done | bytes 327712 | tf_op jit(solution)/shard_map/ppermute | solution.py:363
  61.6 1.3 %coefficients.1 = (f32[32,2,384]{2,1,0:T(2,128)S(1)}, f32[64,64]{1,0:T(8,128)S(1)}, bf16[64,5120]{1,0:T(8,128)(2,1)S(1)}) custom-call(s32[1]{0:T(128)} %bitcast.core_ref, bf16[16,16,640]{2,1,0:T(8,128)(2,1)S(1)} %all_to_all.27.own_ref, bf16[16,16,640]{2,1,0:T(8,128)(2,1)S(1)} %collective-permute-done.1.other_ref, ...), custom_call_target="tpu_custom_call" | custom-call | flops 209715200 | bytes 5000000 | tf_op jit(solution)/shard_map/coefficients/pallas_call | solution.py:227
  62.9 13.4 %all_to_all.28.parts_ref = f32[32,2,384]{2,1,0:T(2,128)S(1)} all-to-all(f32[32,2,384]{2,1,0:T(2,128)S(1)} %get-tuple-element.20), channel_id=1, replica_groups=mesh['y'=4,'z'=8,'x'=4,'core'=2] {'y','z'}, dimensions={0} | all-to-all | bytes 196608 | tf_op jit(solution)/shard_map/all_to_all | solution.py:365
  76.3 0.7 add_up.5
  77.0 3.9 %all-to-all-start.4 = ((f32[32,2,384]{2,1,0:T(2,128)}), f32[32,2,384]{2,1,0:T(2,128)S(1)}, u32[]{:S(2)}, u32[]{:S(2)}) async-start(f32[32,2,384]{2,1,0:T(2,128)} %add_up.5), calls=%async_computation.4 | async-start | bytes 196608 | tf_op jit(solution)/shard_map/all_to_all | solution.py:366
  80.9 6.1 %basis.1 = (f32[64,64]{1,0:T(8,128)S(1)}, bf16[64,5120]{1,0:T(8,128)(2,1)S(1)}) custom-call(f32[64,64]{1,0:T(8,128)S(1)} %get-tuple-element.21.gram_ref, bf16[64,5120]{1,0:T(8,128)(2,1)S(1)} %get-tuple-element.22.sketch_ref), custom_call_target="tpu_custom_call" | custom-call | flops 251658240 | bytes 20000000 | tf_op jit(solution)/shard_map/basis/pallas_call | solution.py:269
  86.9 4.2 %all-to-all-done.4.total_ref = f32[32,2,384]{2,1,0:T(2,128)S(1)} async-done(((f32[32,2,384]{2,1,0:T(2,128)}), f32[32,2,384]{2,1,0:T(2,128)S(1)}, u32[]{:S(2)}, u32[]{:S(2)}) %all-to-all-start.4) | async-done | bytes 98336 | tf_op jit(solution)/shard_map/all_to_all | solution.py:366
  91.1 4.1 %decode.1 = (bf16[320,5120]{1,0:T(8,128)(2,1)}, bf16[320,5120]{1,0:T(8,128)(2,1)}, f32[64,320]{1,0:T(8,128)}) custom-call(f32[32,2,384]{2,1,0:T(2,128)S(1)} %all-to-all-done.4.total_ref, f32[64,64]{1,0:T(8,128)S(1)} %get-tuple-element.23.inverse_ref, bf16[64,5120]{1,0:T(8,128)(2,1)S(1)} %get-tuple-element.24.basis_ref, ...), custom_call_target="tpu_custom_call" | custom-call | flops 209715200 | bytes 10500000 | tf_op jit(solution)/shard_map/decode/pallas_call | solution.py:313
  (1 shorter events, 0.0 us)
Async XLA Ops:
  12.9 1.7 %collective-permute-start = (bf16[16,16,640]{2,1,0:T(8,128)(2,1)S(1)}, bf16[16,16,640]{2,1,0:T(8,128)(2,1)S(1)}, u32[]{:S(2)}, u32[]{:S(2)}) collective-permute-start(bf16[16,16,640]{2,1,0:T(8,128)(2,1)S(1)} %get-tuple-element.17), channel_id=1, source_target_pairs={{0,1},{1,0},{2,3},{3,2},{4,5},{5,4},{6,7},{7,6},{8,9},{9,8},{10,11... | collective-permute-start | bytes 983048 | tf_op jit(solution)/shard_map/ppermute | solution.py:359
  60.0 1.6 %collective-permute-start.1 = (bf16[16,16,640]{2,1,0:T(8,128)(2,1)S(1)}, bf16[16,16,640]{2,1,0:T(8,128)(2,1)S(1)}, u32[]{:S(2)}, u32[]{:S(2)}) collective-permute-start(bf16[16,16,640]{2,1,0:T(8,128)(2,1)S(1)} %all_to_all.27.own_ref), channel_id=1, source_target_pairs={{0,1},{1,0},{2,3},{3,2},{4,5},{5,4},{6,7},{7,6},{8,9},{9,8},{10,11... | collective-permute-start | bytes 983048 | tf_op jit(solution)/shard_map/ppermute | solution.py:363
  77.0 14.1 %all-to-all-start.4 = ((f32[32,2,384]{2,1,0:T(2,128)}), f32[32,2,384]{2,1,0:T(2,128)S(1)}, u32[]{:S(2)}, u32[]{:S(2)}) async-start(f32[32,2,384]{2,1,0:T(2,128)} %add_up.5), calls=%async_computation.4 | async-start | bytes 196608 | tf_op jit(solution)/shard_map/all_to_all | solution.py:366

commit v3 on v2

--- a/solution.py
+++ b/solution.py
@@ -204,51 +204,96 @@
     )(core, *(pltpu.with_memory_space_constraint(x, pltpu.HBM) for x in (grads_t, tokens, memory, warm_t)))
 
 
-def coeff_body(core_ref, own_ref, other_ref, kept_ref, rest_ref, coeff_ref, gram_ref, sketch_ref):
-    core = core_ref[0]
-    for ref, half in ((own_ref, core), (other_ref, 1 - core)):
-        for b in range(HALF // GROUP):
-            for q in range(N_X):
-                at = pl.ds(pl.multiple_of(half * HALF + b * GROUP + q * LANES, LANES), LANES)
-                for p in range(N_Y):
-                    sketch_ref[p * ROWS : (p + 1) * ROWS, at] = ref[q * N_Y + p, :, b * LANES : (b + 1) * LANES]
+def half_terms(half, parts_ref, kept_ref, rest_ref, sketch_ref, total_ref):
+    for b in range(HSTEPS):
+        for q in range(N_X):
+            at = slice(b * GROUP + q * LANES, b * GROUP + (q + 1) * LANES)
+            for p in range(N_Y):
+                sketch_ref[p * ROWS : (p + 1) * ROWS, at] = parts_ref[q * N_Y + p, :, b * LANES : (b + 1) * LANES]
     sketch = sketch_ref[...]
-    gram_ref[...] = lax.dot_general(sketch, sketch, NT, preferred_element_type=F32)
-    coeff = lax.dot_general(sketch[:, :WIDE], kept_ref[...], NT, preferred_element_type=F32)
-    coeff += lax.dot_general(sketch[:, WIDE:], rest_ref[...], NT, preferred_element_type=F32)
+    over = WIDE - HALF
+
+    @pl.when(half == 0)
+    def _():
+        total_ref[...] = lax.dot_general(sketch, kept_ref[:, :HALF], NT, preferred_element_type=F32)
+
+    @pl.when(half == 1)
+    def _():
+        low = lax.dot_general(sketch[:, :over], kept_ref[:, HALF:], NT, preferred_element_type=F32)
+        total_ref[...] = low + lax.dot_general(sketch[:, over:], rest_ref[...], NT, preferred_element_type=F32)
+
+    return lax.dot_general(sketch, sketch, NT, preferred_element_type=F32)
+
+
+def own_body(core_ref, parts_ref, kept_ref, rest_ref, total_ref, gram_ref, sketch_ref):
+    gram_ref[...] = half_terms(core_ref[0], parts_ref, kept_ref, rest_ref, sketch_ref, total_ref)
+
+
+def other_body(
+    core_ref, parts_ref, kept_ref, rest_ref, own_ref, own_gram_ref, coeff_ref, gram_ref, sketch_ref, total_ref
+):
+    gram = half_terms(1 - core_ref[0], parts_ref, kept_ref, rest_ref, sketch_ref, total_ref)
+    gram_ref[...] = gram + own_gram_ref[...]
+    coeff = total_ref[...] + own_ref[...]
     each = R // N_DP
     for i in range(N_DP):
         coeff_ref[i, :, 0:C] = coeff[i * each : (i + 1) * each]
         coeff_ref[i, :, C:] = jnp.zeros((each, PAD - C), F32)
 
 
-def coefficients(core, own, other, kept, rest):
+def own_terms(core, parts, kept, rest):
     vmem = pl.BlockSpec(memory_space=pltpu.VMEM)
     return pl.pallas_call(
-        coeff_body,
+        own_body,
+        out_shape=(
+            jax.ShapeDtypeStruct((R, C), F32),
+            jax.ShapeDtypeStruct((R, R), F32),
+            jax.ShapeDtypeStruct((R, HALF), BF16),
+        ),
+        in_specs=[pl.BlockSpec(memory_space=pltpu.SMEM), vmem, vmem, vmem],
+        out_specs=(vmem, vmem, vmem),
+        compiler_params=pltpu.CompilerParams(vmem_limit_bytes=8 * MIB),
+        cost_estimate=pl.CostEstimate(flops=C * D * R, bytes_accessed=2_500_000, transcendentals=0),
+        name="own_terms",
+    )(core, parts, kept, rest)
+
+
+def coefficients(core, parts, kept, rest, own, own_gram):
+    vmem = pl.BlockSpec(memory_space=pltpu.VMEM)
+    return pl.pallas_call(
+        other_body,
         out_shape=(
             jax.ShapeDtypeStruct((N_DP, R // N_DP, PAD), F32),
             jax.ShapeDtypeStruct((R, R), F32),
-            jax.ShapeDtypeStruct((R, D), BF16),
+            jax.ShapeDtypeStruct((R, HALF), BF16),
         ),
-        in_specs=[pl.BlockSpec(memory_space=pltpu.SMEM), vmem, vmem, vmem, vmem],
+        in_specs=[pl.BlockSpec(memory_space=pltpu.SMEM), vmem, vmem, vmem, vmem, vmem],
         out_specs=(vmem, vmem, vmem),
+        scratch_shapes=[pltpu.VMEM((R, C), F32)],
         compiler_params=pltpu.CompilerParams(vmem_limit_bytes=8 * MIB),
-        cost_estimate=pl.CostEstimate(flops=2 * C * D * R, bytes_accessed=5_000_000, transcendentals=0),
+        cost_estimate=pl.CostEstimate(flops=C * D * R, bytes_accessed=2_500_000, transcendentals=0),
         name="coefficients",
-    )(core, own, other, kept, rest)
-
-
-def basis_body(gram_ref, sketch_ref, inverse_ref, basis_ref):
+    )(core, parts, kept, rest, own, own_gram)
+
+
+def basis_body(core_ref, gram_ref, own_ref, other_ref, inverse_ref, basis_ref):
     row = lax.broadcasted_iota(jnp.int32, (R, R), 0)
     col = lax.broadcasted_iota(jnp.int32, (R, R), 1)
     state = jnp.concatenate([gram_ref[...], (row == col).astype(F32)], axis=1)
     index = lax.broadcasted_iota(jnp.int32, (R, 1), 0)
-    for j in range(R - 1):
-        top = (j + 1) // 8 * 8
-        lead = state[j : j + 1, :]
-        ratio = jnp.where(index[top:] > j, state[top:, j : j + 1] / lead[:, j : j + 1], 0.0)
-        tail = state[top:, :] - ratio * lead
+    spread = lambda x: jnp.broadcast_to(x, (x.shape[0], 2 * R))
+    for j in range(0, R, 2):
+        top = j // 8 * 8
+        lead, second = state[j : j + 1, :], state[j + 1 : j + 2, :]
+        corner, below, last = spread(lead[:, j + 1 : j + 2]), spread(second[:, j : j + 1]), spread(second[:, j + 1 : j + 2])
+        scale = 1.0 / spread(lead[:, j : j + 1])
+        lower = below * scale
+        pivot = 1.0 / (last - lower * corner)
+        left, right = spread(state[top:, j : j + 1]), spread(state[top:, j + 1 : j + 2])
+        right = right - left * (corner * scale)
+        left = jnp.where(index[top:] > j, left, 0.0)
+        right = jnp.where(index[top:] > j + 1, right, 0.0)
+        tail = state[top:, :] - left * (lead * scale) - right * ((second - lower * lead) * pivot)
         state = tail if top == 0 else jnp.concatenate([state[:top], tail], axis=0)
     diagonal = jnp.sum(jnp.where(row == col, state[:, :R], 0.0), axis=1, keepdims=True)
     inverse = state[:, R:] * lax.rsqrt(diagonal)
@@ -257,24 +302,26 @@
     rest = inverse - high.astype(F32)
     middle = rest.astype(BF16)
     low = (rest - middle.astype(F32)).astype(BF16)
-    sketch = sketch_ref[...]
-    out = jnp.dot(high, sketch, preferred_element_type=F32)
-    out += jnp.dot(middle, sketch, preferred_element_type=F32)
-    out += jnp.dot(low, sketch, preferred_element_type=F32)
-    basis_ref[...] = out.astype(BF16)
-
-
-def basis(gram, sketch_t):
+    core = core_ref[0]
+    for ref, half in ((own_ref, core), (other_ref, 1 - core)):
+        sketch = ref[...]
+        out = jnp.dot(high, sketch, preferred_element_type=F32)
+        out += jnp.dot(middle, sketch, preferred_element_type=F32)
+        out += jnp.dot(low, sketch, preferred_element_type=F32)
+        basis_ref[:, pl.ds(pl.multiple_of(half * HALF, LANES), HALF)] = out.astype(BF16)
+
+
+def basis(core, gram, own, other):
     vmem = pl.BlockSpec(memory_space=pltpu.VMEM)
     return pl.pallas_call(
         basis_body,
         out_shape=(jax.ShapeDtypeStruct((R, R), F32), jax.ShapeDtypeStruct((R, D), BF16)),
-        in_specs=[vmem, vmem],
+        in_specs=[pl.BlockSpec(memory_space=pltpu.SMEM), vmem, vmem, vmem],
         out_specs=(vmem, vmem),
         compiler_params=pltpu.CompilerParams(vmem_limit_bytes=8 * MIB),
         cost_estimate=pl.CostEstimate(flops=2 * R * R * D * 6, bytes_accessed=20_000_000, transcendentals=0),
         name="basis",
-    )(gram, sketch_t)
+    )(core, gram, own, other)
 
 
 def decode_body(
@@ -287,21 +334,40 @@
     start = jnp.dot(inverse_ref[...], total, precision=lax.Precision.HIGHEST, preferred_element_type=F32) * (1.0 / N_DP)
     start_ref[...] = start
     half = start.astype(BF16).T
-    copies = []
-    for j in range(DSTEPS):
-        at = pl.ds(j * DBLK, DBLK)
-        if j * DBLK == WIDE:
-            rest_copy.wait()
-        merged = kept_ref[:, at] if j * DBLK < WIDE else rest[:, j * DBLK - WIDE : (j + 1) * DBLK - WIDE]
+
+    def copies(j):
+        at = pl.ds(pl.multiple_of(j * DBLK, DBLK), DBLK)
+        return (
+            pltpu.make_async_copy(update.at[:, at], update_hbm.at[:, at], update_sem.at[j]),
+            pltpu.make_async_copy(error.at[:, at], error_hbm.at[:, at], error_sem.at[j]),
+        )
+
+    def block(j, source, base):
+        at = pl.ds(pl.multiple_of(j * DBLK, DBLK), DBLK)
+        of = pl.ds(pl.multiple_of(j * DBLK - base, DBLK), DBLK)
         decoded = jnp.dot(half, basis_ref[:, at], preferred_element_type=F32)
         update[:, at] = decoded.astype(BF16)
-        error[:, at] = (merged.astype(F32) - decoded).astype(BF16)
-        copies.append(pltpu.make_async_copy(update.at[:, at], update_hbm.at[:, at], update_sem.at[j]))
-        copies.append(pltpu.make_async_copy(error.at[:, at], error_hbm.at[:, at], error_sem.at[j]))
-        copies[-2].start()
-        copies[-1].start()
-    for copy in copies:
-        copy.wait()
+        error[:, at] = (source[:, of].astype(F32) - decoded).astype(BF16)
+        for copy in copies(j):
+            copy.start()
+
+    def from_kept(j, carry):
+        block(j, kept_ref, 0)
+        return carry
+
+    def from_rest(j, carry):
+        block(j, rest, WIDE)
+        return carry
+
+    def drain(j, carry):
+        for copy in copies(j):
+            copy.wait()
+        return carry
+
+    lax.fori_loop(0, WIDE // DBLK, from_kept, 0)
+    rest_copy.wait()
+    lax.fori_loop(WIDE // DBLK, DSTEPS, from_rest, 0)
+    lax.fori_loop(0, DSTEPS, drain, 0)
 
 
 DBLK = 1024
@@ -359,12 +425,13 @@
     mine = (own + lax.ppermute(send, "core", swap).astype(F32)).astype(BF16)
     parts = lax.all_to_all(mine, ("y", "x"), 0, 0, tiled=True)
     parts = lax.all_to_all(add_up(parts, N_Z), "z", 0, 0, tiled=True)
-    sketch_own = lax.all_to_all(add_up(parts, PARTS), ("y", "x"), 0, 0, tiled=True)
-    sketch_other = lax.ppermute(sketch_own, "core", swap)
-    coeff, gram, sketch_t = coefficients(core, sketch_own, sketch_other, kept, rest)
+    parts_own = lax.all_to_all(add_up(parts, PARTS), ("y", "x"), 0, 0, tiled=True)
+    parts_other = lax.ppermute(parts_own, "core", swap)
+    own_total, own_gram, sketch_own = own_terms(core, parts_own, kept, rest)
+    coeff, gram, sketch_other = coefficients(core, parts_other, kept, rest, own_total, own_gram)
     terms = lax.all_to_all(coeff, ("y", "z"), 0, 0, tiled=True)
     total = lax.all_to_all(add_up(terms, N_DP), ("y", "z"), 0, 0, tiled=True)
-    inverse, basis_t = basis(gram, sketch_t)
+    inverse, basis_t = basis(core, gram, sketch_own, sketch_other)
     update, new_error, start_t = decode(total, inverse, basis_t, kept, rest_hbm)
     return update, new_error[None], start_t.T
 

time: 95.6 us -> 95.1 us (level)
  Pallas kernels: 24.6 us -> 23 us
  waiting for transfers between devices: 7.43 us -> 8.56 us
    pallas_call x1, Pallas kernels: 6.08 us -> 4.03 us  [basis(): pl.pallas_call(basis_body, out_shape=(jax.ShapeDtypeStruct((R, R), F32),...]
    all_to_all x1, waiting for transfers between devices: 4.18 us -> 6.23 us  [per_device(): total = lax.all_to_all(add_up(terms, N_DP), ('y', 'z'), 0, 0, tiled=True)]
  transfers between devices with their start and end apart: 3 -> 3, of which waited for: 3 -> 3; matrix products, arithmetic and copies ran while one was open for 0% -> 0% of each run, Pallas kernels for 6% -> 5%
where the time goes in v3:
time: 95.1 us; the launch traced here: 94.8 us
  blocking collectives  58.5 us (62%)
  Pallas kernels  23 us (24%)
  waiting for transfers between devices  8.56 us (9%)
  starting transfers between devices  3.95 us (4%)
    all_to_all x1, blocking collectives, per_device(): parts = lax.all_to_all(add_up(parts, N_Z), 'z', 0, 0, tiled=True)  17.7 us
    all_to_all x1, blocking collectives, per_device(): parts = lax.all_to_all(mine, ('y', 'x'), 0, 0, tiled=True)  15.6 us
    all_to_all x1, blocking collectives, per_device(): terms = lax.all_to_all(coeff, ('y', 'z'), 0, 0, tiled=True)  13.4 us
    pallas_call x1, Pallas kernels, merge(): pl.pallas_call(merge_body, out_shape=(jax.ShapeDtypeStruct((C, WIDE), BF1...  12.3 us
    all_to_all x1, blocking collectives, per_device(): lax.all_to_all(add_up(parts, PARTS), ('y', 'x'), 0, 0, tiled=True)  11.9 us
    all_to_all x1, waiting for transfers between devices, per_device(): total = lax.all_to_all(add_up(terms, N_DP), ('y', 'z'), 0, 0, tiled=True)  6.23 us
    pallas_call x1, Pallas kernels, decode(): pl.pallas_call(decode_body, out_shape=(jax.ShapeDtypeStruct((C, D), BF16)...  4.11 us
    pallas_call x1, Pallas kernels, basis(): pl.pallas_call(basis_body, out_shape=(jax.ShapeDtypeStruct((R, R), F32),...  4.03 us
  transfers between devices with their start and end apart: 3, of which 3 were waited for; matrix products, arithmetic and copies ran while one was open for 0% of the time, Pallas kernels for 5%

profile of v3, /device:TPU:2, one launch (start us, length us, event | category | flops | bytes accessed | tf_op | source)
XLA Modules:
  0.0 94.8 jit_solution(2596916718869644208)
XLA Ops:
  0.6 12.3 %merge.1 = (bf16[320,3072]{1,0:T(8,128)(2,1)S(1)}, bf16[320,2048]{1,0:T(8,128)(2,1)S(1)}, bf16[320,2048]{1,0:T(8,128)(2,1)}, bf16[16,16,640]{2,1,0:T(8,128)(2,1)S(1)}, f32[16,16,640]{2,1,0:T(8,128)S(1)}) custom-call(s32[1]{0:T(128)} %bitcast.core_ref, bf16[320,2048]{1,0:T(8,128)(2,1)} %bitcast.8, bf16[2048,5120]{1,0:T(8,128)(2,1)} %tokens_hbm.1, ...), custom_call_target="tpu_custom_call" | custom-call | flops 6920601600 | bytes 30000000 | tf_op jit(solution)/shard_map/merge/pallas_call | solution.py:176
  12.9 0.1 collective-permute-start
  13.0 1.6 %collective-permute-done = bf16[16,16,640]{2,1,0:T(8,128)(2,1)S(1)} collective-permute-done((bf16[16,16,640]{2,1,0:T(8,128)(2,1)S(1)}, bf16[16,16,640]{2,1,0:T(8,128)(2,1)S(1)}, u32[]{:S(2)}, u32[]{:S(2)}) %collective-permute-start) | collective-permute-done | bytes 327712 | tf_op jit(solution)/shard_map/ppermute | solution.py:425
  14.6 0.1 add_convert_fusion
  14.7 15.6 %all_to_all.25.parts_ref = bf16[16,16,640]{2,1,0:T(8,128)(2,1)S(1)} all-to-all(bf16[16,16,640]{2,1,0:T(8,128)(2,1)S(1)} %add_convert_fusion), channel_id=1, replica_groups=mesh['y'=4,'z'=8,'x'=4,'core'=2] {'y','x'}, dimensions={0} | all-to-all | bytes 655360 | tf_op jit(solution)/shard_map/all_to_all | solution.py:426
  30.3 0.1 add_up.3
  30.3 17.7 %all_to_all.26.parts_ref = bf16[8,16,640]{2,1,0:T(8,128)(2,1)S(1)} all-to-all(bf16[8,16,640]{2,1,0:T(8,128)(2,1)S(1)} %add_up.3), channel_id=1, replica_groups=mesh['y'=4,'z'=8,'x'=4,'core'=2] {'z'}, dimensions={0} | all-to-all | bytes 327680 | tf_op jit(solution)/shard_map/all_to_all | solution.py:427
  48.0 11.9 %all_to_all.27.parts_ref = bf16[16,16,640]{2,1,0:T(8,128)(2,1)S(1)} all-to-all(bf16[16,16,640]{2,1,0:T(8,128)(2,1)S(1)} %add_up.4), channel_id=1, replica_groups=mesh['y'=4,'z'=8,'x'=4,'core'=2] {'y','x'}, dimensions={0} | all-to-all | bytes 655360 | tf_op jit(solution)/shard_map/all_to_all | solution.py:428
  60.0 0.0 collective-permute-start.1
  60.0 0.9 own_terms.1
  60.9 0.7 collective-permute-done.1.parts_ref
  61.6 0.9 coefficients.1
  62.5 13.4 %all_to_all.28.parts_ref = f32[32,2,384]{2,1,0:T(2,128)S(1)} all-to-all(f32[32,2,384]{2,1,0:T(2,128)S(1)} %get-tuple-element.25), channel_id=1, replica_groups=mesh['y'=4,'z'=8,'x'=4,'core'=2] {'y','z'}, dimensions={0} | all-to-all | bytes 196608 | tf_op jit(solution)/shard_map/all_to_all | solution.py:432
  75.9 0.7 add_up.5
  76.6 3.9 %all-to-all-start.4 = ((f32[32,2,384]{2,1,0:T(2,128)}), f32[32,2,384]{2,1,0:T(2,128)S(1)}, u32[]{:S(2)}, u32[]{:S(2)}) async-start(f32[32,2,384]{2,1,0:T(2,128)} %add_up.5), calls=%async_computation.4 | async-start | bytes 196608 | tf_op jit(solution)/shard_map/all_to_all | solution.py:433
  80.4 4.0 %basis.1 = (f32[64,64]{1,0:T(8,128)S(1)}, bf16[64,5120]{1,0:T(8,128)(2,1)S(1)}) custom-call(s32[1]{0:T(128)} %bitcast.core_ref, f32[64,64]{1,0:T(8,128)S(1)} %get-tuple-element.26.gram_ref, bf16[64,2560]{1,0:T(8,128)(2,1)S(1)} %get-tuple-element.27.own_ref, bf16[64,2560]{1,0:T(8,128)(2,1)S(1)} %get-tuple-element.28.other_ref), custom_call_target="tpu_custom_call" | custom-call | flops 251658240 | bytes 20000000 | tf_op jit(solution)/shard_map/basis/pallas_call | solution.py:316
  84.5 6.2 %all-to-all-done.4.total_ref = f32[32,2,384]{2,1,0:T(2,128)S(1)} async-done(((f32[32,2,384]{2,1,0:T(2,128)}), f32[32,2,384]{2,1,0:T(2,128)S(1)}, u32[]{:S(2)}, u32[]{:S(2)}) %all-to-all-start.4) | async-done | bytes 98336 | tf_op jit(solution)/shard_map/all_to_all | solution.py:433
  90.7 4.1 %decode.1 = (bf16[320,5120]{1,0:T(8,128)(2,1)}, bf16[320,5120]{1,0:T(8,128)(2,1)}, f32[64,320]{1,0:T(8,128)}) custom-call(f32[32,2,384]{2,1,0:T(2,128)S(1)} %all-to-all-done.4.total_ref, f32[64,64]{1,0:T(8,128)S(1)} %get-tuple-element.29.inverse_ref, bf16[64,5120]{1,0:T(8,128)(2,1)S(1)} %get-tuple-element.30.basis_ref, ...), custom_call_target="tpu_custom_call" | custom-call | flops 209715200 | bytes 10500000 | tf_op jit(solution)/shard_map/decode/pallas_call | solution.py:379
  (1 shorter events, 0.0 us)
Async XLA Ops:
  12.9 1.7 %collective-permute-start = (bf16[16,16,640]{2,1,0:T(8,128)(2,1)S(1)}, bf16[16,16,640]{2,1,0:T(8,128)(2,1)S(1)}, u32[]{:S(2)}, u32[]{:S(2)}) collective-permute-start(bf16[16,16,640]{2,1,0:T(8,128)(2,1)S(1)} %get-tuple-element.20), channel_id=1, source_target_pairs={{0,1},{1,0},{2,3},{3,2},{4,5},{5,4},{6,7},{7,6},{8,9},{9,8},{10,11... | collective-permute-start | bytes 983048 | tf_op jit(solution)/shard_map/ppermute | solution.py:425
  60.0 1.6 %collective-permute-start.1 = (bf16[16,16,640]{2,1,0:T(8,128)(2,1)S(1)}, bf16[16,16,640]{2,1,0:T(8,128)(2,1)S(1)}, u32[]{:S(2)}, u32[]{:S(2)}) collective-permute-start(bf16[16,16,640]{2,1,0:T(8,128)(2,1)S(1)} %all_to_all.27.parts_ref), channel_id=1, source_target_pairs={{0,1},{1,0},{2,3},{3,2},{4,5},{5,4},{6,7},{7,6},{8,9},{9,8},{10,11... | collective-permute-start | bytes 983048 | tf_op jit(solution)/shard_map/ppermute | solution.py:429
  76.6 14.1 %all-to-all-start.4 = ((f32[32,2,384]{2,1,0:T(2,128)}), f32[32,2,384]{2,1,0:T(2,128)S(1)}, u32[]{:S(2)}, u32[]{:S(2)}) async-start(f32[32,2,384]{2,1,0:T(2,128)} %add_up.5), calls=%async_computation.4 | async-start | bytes 196608 | tf_op jit(solution)/shard_map/all_to_all | solution.py:433
